TPU v7x, 512 devices: a whole 4x4x16 slice. The times are simulated.
512 devices in a mesh: gx: 32 (over x, z_lo, core), gy: 16 (over y, z_hi).
Axes of the slice: x: 4, y: 4, z: 16 (z_hi: 4, z_lo: 4; z = z_hi * 4 + z_lo), core: 2. Of those that a mesh axis runs over, the one named last changes fastest.
Arguments:
- state_field: float32 [128, 128, 2304], P('gx', 'gy'), may hold values from -6 to 6
- conv_first: float32 [3, 3, 36, 108], replicated, may hold values from -0.1875 to 0.1875
- conv_second: float32 [3, 3, 36, 108], replicated, may hold values from -0.1875 to 0.1875
- spec_real: float32 [32, 32, 36, 432], P('gx', 'gy'), may hold values from -12 to 12
- spec_imag: float32 [32, 32, 36, 432], P('gx', 'gy'), may hold values from -12 to 12
Outputs:
- layer_out: float32 [128, 128, 2304], P('gx', 'gy')
All inputs are finite; a program needn't handle non-finite values.
Results may differ from a plain program's by a relative error of at most 0.00007.
Values sent between devices are 32-bit elements; how exact they have to be, the bound alone decides.
A program may use at most 128 MiB of HBM per device.

v0:
```python
import jax
import jax.numpy as jnp
from jax import lax
from jax.sharding import PartitionSpec as P

C = 36
Z = 64
MX = 16
MY = 16
MZ = 12
highest = lax.Precision.HIGHEST
two_pi = 6.283185307179586


def with_halo(cells, sides, width):
    for axis, dim in sides:
        count = lax.axis_size(axis)
        ends = count - 1
        head = lax.slice_in_dim(cells, 0, width, axis=dim)
        tail = lax.slice_in_dim(cells, cells.shape[dim] - width, cells.shape[dim], axis=dim)
        cells = jnp.concatenate(
            [
                lax.ppermute(tail, axis, [(i, (i + 1) % count) for i in range(ends)]),
                cells,
                lax.ppermute(head, axis, [((i + 1) % count, i) for i in range(ends)]),
            ],
            axis=dim,
        )
    return cells


def matmul(left, right):
    return jnp.dot(left, right, precision=highest)


def kept_modes(mode_count, length):
    places = jnp.arange(2 * mode_count, dtype=jnp.int32)
    return jnp.where(places < mode_count, places, places + length - 2 * mode_count)


def angle_table(first_index, second_index, length):
    product = first_index[:, None] * second_index[None, :] % length
    angles = product.astype(jnp.float32) * (two_pi / length)
    return (jnp.cos(angles), jnp.sin(angles))


def convolve(extended, kernel, rows_out, cols_out):
    shaped = extended.reshape(rows_out + 2, cols_out + 2, C, Z)
    moved = jnp.transpose(shaped, (2, 0, 1, 3))
    padded = jnp.pad(moved, ((0, 0), (0, 0), (0, 0), (1, 1)))
    summed = jnp.zeros((C, rows_out * cols_out * Z), jnp.float32)
    for shift_x in range(3):
        for shift_y in range(3):
            for shift_z in range(3):
                window = padded[
                    :,
                    shift_x : shift_x + rows_out,
                    shift_y : shift_y + cols_out,
                    shift_z : shift_z + Z,
                ]
                block = kernel[shift_x, shift_y, :, shift_z * C : (shift_z + 1) * C]
                summed = summed + matmul(block, window.reshape(C, rows_out * cols_out * Z))
    return jnp.transpose(summed.reshape(C, rows_out, cols_out, Z), (1, 2, 0, 3))


def on_device(state_field, conv_first, conv_second, spec_real, spec_imag):
    rows_here = state_field.shape[0]
    cols_here = state_field.shape[1]
    total_x = rows_here * lax.axis_size("gx")
    total_y = cols_here * lax.axis_size("gy")
    row_start = lax.axis_index("gx") * rows_here
    col_start = lax.axis_index("gy") * cols_here
    chan_modes = C * MZ
    width_q = cols_here * chan_modes
    extended = with_halo(state_field, (("gx", 0), ("gy", 1)), 1)
    hidden_field = jax.nn.gelu(
        convolve(extended, conv_first, rows_here, cols_here), approximate=False
    )
    hidden_rim = with_halo(
        hidden_field.reshape(rows_here, cols_here, C * Z), (("gx", 0), ("gy", 1)), 1
    )
    conv_out = convolve(hidden_rim, conv_second, rows_here, cols_here)
    z_cells = jnp.arange(Z, dtype=jnp.int32)
    z_freqs = jnp.arange(MZ, dtype=jnp.int32)
    z_cosine, z_sine = angle_table(z_cells, z_freqs, Z)
    flat_cells = state_field.reshape(rows_here * cols_here * C, Z)
    z_real = matmul(flat_cells, z_cosine).reshape(rows_here, width_q)
    z_imag = -matmul(flat_cells, z_sine).reshape(rows_here, width_q)
    x_freqs = kept_modes(MX, total_x)
    local_x = row_start + jnp.arange(rows_here, dtype=jnp.int32)
    frequency = x_freqs
    cosine, sine_part = angle_table(frequency, local_x, total_x)
    term_real = matmul(cosine, z_real) + matmul(sine_part, z_imag)
    term_imag = matmul(cosine, z_imag) - matmul(sine_part, z_real)
    joined = lax.psum_scatter(
        jnp.concatenate([term_real, term_imag], axis=1), "gx", scatter_dimension=0, tiled=True
    )
    mode_real = joined[:, :width_q]
    mode_imag = joined[:, width_q:]
    kxd_rows = mode_real.shape[0]
    y_real = mode_real.reshape(kxd_rows, cols_here, chan_modes)
    y_imag = mode_imag.reshape(kxd_rows, cols_here, chan_modes)
    y_freqs = kept_modes(MY, total_y)
    local_y = col_start + jnp.arange(cols_here, dtype=jnp.int32)
    frequency = y_freqs
    cosine, sine_part = angle_table(frequency, local_y, total_y)
    term_real = jnp.einsum("my,ayq->maq", cosine, y_real, precision=highest) + jnp.einsum(
        "my,ayq->maq", sine_part, y_imag, precision=highest
    )
    term_imag = jnp.einsum("my,ayq->maq", cosine, y_imag, precision=highest) - jnp.einsum(
        "my,ayq->maq", sine_part, y_real, precision=highest
    )
    owned = lax.psum_scatter(
        jnp.concatenate([term_real, term_imag], axis=2), "gy", scatter_dimension=0, tiled=True
    )
    kyd_rows = owned.shape[0]
    owned_real = owned[..., :chan_modes].reshape(kyd_rows, kxd_rows, C, MZ)
    owned_imag = owned[..., chan_modes:].reshape(kyd_rows, kxd_rows, C, MZ)
    weight_real = spec_real.reshape(kxd_rows, kyd_rows, C, MZ, C)
    weight_imag = spec_imag.reshape(kxd_rows, kyd_rows, C, MZ, C)
    mixed_real = jnp.einsum(
        "baik,abiko->baok", owned_real, weight_real, precision=highest
    ) - jnp.einsum("baik,abiko->baok", owned_imag, weight_imag, precision=highest)
    mixed_imag = jnp.einsum(
        "baik,abiko->baok", owned_real, weight_imag, precision=highest
    ) + jnp.einsum("baik,abiko->baok", owned_imag, weight_real, precision=highest)
    mixed = jnp.concatenate(
        [
            mixed_real.reshape(kyd_rows, kxd_rows, chan_modes),
            mixed_imag.reshape(kyd_rows, kxd_rows, chan_modes),
        ],
        axis=2,
    )
    shard_piece = lax.all_gather(mixed, "gy", axis=0, tiled=True)
    frequency = y_freqs
    cosine, sine_part = angle_table(local_y, frequency, total_y)
    piece_real = shard_piece[..., :chan_modes]
    piece_imag = shard_piece[..., chan_modes:]
    add_real = jnp.einsum("ym,maq->ayq", cosine, piece_real, precision=highest) - jnp.einsum(
        "ym,maq->ayq", sine_part, piece_imag, precision=highest
    )
    add_imag = jnp.einsum("ym,maq->ayq", cosine, piece_imag, precision=highest) + jnp.einsum(
        "ym,maq->ayq", sine_part, piece_real, precision=highest
    )
    returned = jnp.concatenate([add_real, add_imag], axis=2)
    back_real = returned[..., :chan_modes].reshape(kxd_rows, width_q)
    back_imag = returned[..., chan_modes:].reshape(kxd_rows, width_q)
    joined_back = jnp.concatenate([back_real, back_imag], axis=1)
    shard_piece = lax.all_gather(joined_back, "gx", axis=0, tiled=True)
    frequency = x_freqs
    cosine, sine_part = angle_table(local_x, frequency, total_x)
    piece_real = shard_piece[:, :width_q]
    piece_imag = shard_piece[:, width_q:]
    add_real = matmul(cosine, piece_real) - matmul(sine_part, piece_imag)
    add_imag = matmul(cosine, piece_imag) + matmul(sine_part, piece_real)
    gathered = jnp.concatenate([add_real, add_imag], axis=1)
    cell_real = gathered[:, :width_q]
    cell_imag = gathered[:, width_q:]
    scaling = 1.0 / (total_x * total_y * Z)
    factors = jnp.where(z_freqs == 0, 1.0, 2.0).astype(jnp.float32) * scaling
    back_cosine, back_sine = angle_table(z_freqs, z_cells, Z)
    back_cosine = back_cosine * factors[:, None]
    back_sine = back_sine * factors[:, None]
    spectral = matmul(cell_real.reshape(rows_here * cols_here * C, MZ), back_cosine) - matmul(
        cell_imag.reshape(rows_here * cols_here * C, MZ), back_sine
    )
    spectral = spectral.reshape(rows_here, cols_here, C, Z)
    layer_out = jax.nn.gelu(spectral + conv_out, approximate=False)
    return layer_out.reshape(rows_here, cols_here, C * Z)


def solution(mesh):
    in_specs = (P("gx", "gy", None), P(), P(), P("gx", "gy", None, None), P("gx", "gy", None, None))
    out_specs = P("gx", "gy", None)
    return jax.shard_map(
        on_device, mesh=mesh, in_specs=in_specs, out_specs=out_specs, check_vma=False
    )
```

profile of v0, /device:TPU:1, one launch (start us, length us, event | category | flops | bytes accessed | tf_op | source)
XLA Modules:
  0.0 637.4 jit_solution(1770213632262422438)
XLA Ops:
  7.5 8.8 %collective-permute-start.1 = (f32[1,8,2304]{2,1,0:T(8,128)S(1)}, f32[1,8,2304]{2,1,0:T(8,128)S(1)}, u32[]{:S(2)}, u32[]{:S(2)}) collective-permute-start(f32[1,8,2304]{2,1,0:T(8,128)S(1)} %get-tuple-element.75), channel_id=1, source_target_pairs={{16,0},{32,16},{48,32},{64,48},{80,64},{96,80},{112,96},{128,112},... | collective-permute-start | bytes 221192 | tf_op jit(solution)/shard_map/ppermute | solution.py:25
  24.9 5.0 collective-permute-start.2
  32.8 10.6 %collective-permute-done.3 = f32[6,1,2304]{2,1,0:T(1,128)S(1)} collective-permute-done((f32[6,1,2304]{2,1,0:T(1,128)S(1)}, f32[6,1,2304]{2,1,0:T(1,128)S(1)}, u32[]{:S(2)}, u32[]{:S(2)}) %collective-permute-start.3) | collective-permute-done | bytes 55328 | tf_op jit(solution)/shard_map/ppermute | solution.py:25
  46.2 4.3 pad_slice_fusion.24
  50.5 3.8 fusion.326
  85.3 2.0 reshape.344
  101.5 2.1 fusion.130
  103.6 2.2 convolution_bitcast_fusion.11
  121.0 2.2 convolution_bitcast_fusion.16
  124.5 2.1 convolution_bitcast_fusion.15
  127.9 2.2 convolution_bitcast_fusion.13
  151.6 2.4 collective-permute-start.5
  154.1 3.6 collective-permute-done.5
  157.8 8.5 %collective-permute-start.6 = (f32[6,1,2304]{2,1,0:T(1,128)S(1)}, f32[6,1,2304]{2,1,0:T(1,128)S(1)}, u32[]{:S(2)}, u32[]{:S(2)}) collective-permute-start(f32[6,1,2304]{2,1,0:T(1,128)S(1)} %get-tuple-element.69), channel_id=1, source_target_pairs={{0,1},{1,2},{2,3},{3,4},{4,5},{5,6},{6,7},{7,8},{8,9},{9,10},{10,1... | collective-permute-start | bytes 165896 | tf_op jit(solution)/shard_map/ppermute | solution.py:23
  173.5 4.0 collective-permute-done.7
  180.4 4.3 pad_slice_fusion.6
  184.6 3.8 fusion.324
  200.4 2.0 reshape.368
  236.9 2.1 fusion.102
  241.4 2.0 reshape.383
  280.7 38.4 %all-reduce.7.cloned.1.call-done = f32[32,6912]{1,0:T(8,128)} async-done(((f32[32,6912]{1,0:T(8,128)}), f32[32,6912]{1,0:T(8,128)}) %all-reduce.7.cloned.1.call-update) | async-done | bytes 884752
  325.2 188.3 %all-reduce.9.cloned.1.call-done = f32[32,1,864]{2,0,1:T(8,128)} async-done(((f32[32,1,864]{2,0,1:T(8,128)}), f32[32,1,864]{2,0,1:T(8,128)}) %all-reduce.9.cloned.1.call-update) | async-done | bytes 110608
  515.8 42.2 %all_gather.6 = f32[32,1,864]{2,1,0:T(1,128)S(1)} all-gather(f32[2,1,864]{2,1,0:T(1,128)S(1)} %copy.74), channel_id=1, replica_groups=mesh['gx'=32,'gy'=16] {'gy'}, dimensions={0}, use_global_device_ids=true | all-gather | bytes 117504 | tf_op jit(solution)/shard_map/all_gather | solution.py:134
  559.5 63.2 %all-gather = f32[32,1,6912]{2,1,0:T(1,128)S(1)} all-gather(f32[1,1,6912]{2,1,0:T(1,128)S(1)} %maximum_bitcast_fusion), channel_id=1, replica_groups=mesh['gx'=32,'gy'=16] {'gx'}, dimensions={0}, use_global_device_ids=true | all-gather | bytes 912384 | tf_op jit(solution)/shard_map/all_gather | solution.py:149
  (460 shorter events, 211.4 us)
Async XLA Ops:
  6.5 312.6 %all-reduce.7.cloned.1.call-start = ((), (), s32[]{:S(2)}) async-start(), calls=%async_computation | async-start | bytes 1769472
  7.5 17.3 %collective-permute-start.1 = (f32[1,8,2304]{2,1,0:T(8,128)S(1)}, f32[1,8,2304]{2,1,0:T(8,128)S(1)}, u32[]{:S(2)}, u32[]{:S(2)}) collective-permute-start(f32[1,8,2304]{2,1,0:T(8,128)S(1)} %get-tuple-element.75), channel_id=1, source_target_pairs={{16,0},{32,16},{48,32},{64,48},{80,64},{96,80},{112,96},{128,112},... | collective-permute-start | bytes 221192 | tf_op jit(solution)/shard_map/ppermute | solution.py:25
  16.3 8.5 %collective-permute-start = (f32[1,8,2304]{2,1,0:T(8,128)S(1)}, f32[1,8,2304]{2,1,0:T(8,128)S(1)}, u32[]{:S(2)}, u32[]{:S(2)}) collective-permute-start(f32[1,8,2304]{2,1,0:T(8,128)S(1)} %get-tuple-element.76), channel_id=1, source_target_pairs={{0,16},{16,32},{32,48},{48,64},{64,80},{80,96},{96,112},{112,128},... | collective-permute-start | bytes 221192 | tf_op jit(solution)/shard_map/ppermute | solution.py:23
  24.9 7.9 %collective-permute-start.2 = (f32[6,1,2304]{2,1,0:T(1,128)S(1)}, f32[6,1,2304]{2,1,0:T(1,128)S(1)}, u32[]{:S(2)}, u32[]{:S(2)}) collective-permute-start(f32[6,1,2304]{2,1,0:T(1,128)S(1)} %get-tuple-element.71), channel_id=1, source_target_pairs={{0,1},{1,2},{2,3},{3,4},{4,5},{5,6},{6,7},{7,8},{8,9},{9,10},{10,1... | collective-permute-start | bytes 165896 | tf_op jit(solution)/shard_map/ppermute | solution.py:23
  29.9 13.5 %collective-permute-start.3 = (f32[6,1,2304]{2,1,0:T(1,128)S(1)}, f32[6,1,2304]{2,1,0:T(1,128)S(1)}, u32[]{:S(2)}, u32[]{:S(2)}) collective-permute-start(f32[6,1,2304]{2,1,0:T(1,128)S(1)} %get-tuple-element.72), channel_id=1, source_target_pairs={{1,0},{2,1},{3,2},{4,3},{5,4},{6,5},{7,6},{8,7},{9,8},{10,9},{11,1... | collective-permute-start | bytes 165896 | tf_op jit(solution)/shard_map/ppermute | solution.py:25
  32.2 481.3 %all-reduce.9.cloned.1.call-start = ((), (), s32[]{:S(2)}) async-start(), calls=%async_computation.1 | async-start | bytes 229376
  100.5 5.3 copy-start.14
  149.3 21.2 %copy-start.100 = (f32[1,2,36,432]{3,1,2,0:T(2,128)S(1)}, f32[1,2,36,432]{3,1,2,0:T(2,128)}, u32[]{:S(2)}) copy-start(f32[1,2,36,432]{3,1,2,0:T(2,128)} %param.8) | copy-start | bytes 373252
  149.4 4.6 collective-permute-start.4
  151.5 20.2 %copy-start.101 = (f32[1,2,36,432]{3,1,2,0:T(2,128)S(1)}, f32[1,2,36,432]{3,1,2,0:T(2,128)}, u32[]{:S(2)}) copy-start(f32[1,2,36,432]{3,1,2,0:T(2,128)} %param.9) | copy-start | bytes 373252
  151.6 6.1 collective-permute-start.5
  157.8 15.7 %collective-permute-start.6 = (f32[6,1,2304]{2,1,0:T(1,128)S(1)}, f32[6,1,2304]{2,1,0:T(1,128)S(1)}, u32[]{:S(2)}, u32[]{:S(2)}) collective-permute-start(f32[6,1,2304]{2,1,0:T(1,128)S(1)} %get-tuple-element.69), channel_id=1, source_target_pairs={{0,1},{1,2},{2,3},{3,4},{4,5},{5,6},{6,7},{7,8},{8,9},{9,10},{10,1... | collective-permute-start | bytes 165896 | tf_op jit(solution)/shard_map/ppermute | solution.py:23
  166.3 11.2 %collective-permute-start.7 = (f32[6,1,2304]{2,1,0:T(1,128)S(1)}, f32[6,1,2304]{2,1,0:T(1,128)S(1)}, u32[]{:S(2)}, u32[]{:S(2)}) collective-permute-start(f32[6,1,2304]{2,1,0:T(1,128)S(1)} %get-tuple-element.70), channel_id=1, source_target_pairs={{1,0},{2,1},{3,2},{4,3},{5,4},{6,5},{7,6},{8,7},{9,8},{10,9},{11,1... | collective-permute-start | bytes 165896 | tf_op jit(solution)/shard_map/ppermute | solution.py:25
  235.5 4.7 copy-start.15
  279.0 44.1 %copy-start.58 = (f32[36,2048]{1,0:T(8,128)S(1)}, f32[36,2048]{1,0:T(8,128)}, u32[]{:S(2)}) copy-start(f32[36,2048]{1,0:T(8,128)} %convolution_bitcast_fusion.3) | copy-start | bytes 884740
  279.0 44.1 %copy-start.59 = (f32[36,2048]{1,0:T(8,128)S(1)}, f32[36,2048]{1,0:T(8,128)}, u32[]{:S(2)}) copy-start(f32[36,2048]{1,0:T(8,128)} %convolution_bitcast_fusion.2) | copy-start | bytes 884740
  279.0 44.1 %copy-start.60 = (f32[36,2048]{1,0:T(8,128)S(1)}, f32[36,2048]{1,0:T(8,128)}, u32[]{:S(2)}) copy-start(f32[36,2048]{1,0:T(8,128)} %convolution_bitcast_fusion) | copy-start | bytes 884740
  279.4 43.7 %copy-start.51 = (f32[36,2048]{1,0:T(8,128)S(1)}, f32[36,2048]{1,0:T(8,128)}, u32[]{:S(2)}) copy-start(f32[36,2048]{1,0:T(8,128)} %reshape.384) | copy-start | bytes 884740
  279.4 43.7 %copy-start.53 = (f32[36,2048]{1,0:T(8,128)S(1)}, f32[36,2048]{1,0:T(8,128)}, u32[]{:S(2)}) copy-start(f32[36,2048]{1,0:T(8,128)} %convolution_bitcast_fusion.1) | copy-start | bytes 884740
  279.5 43.7 %copy-start.54 = (f32[36,2048]{1,0:T(8,128)S(1)}, f32[36,2048]{1,0:T(8,128)}, u32[]{:S(2)}) copy-start(f32[36,2048]{1,0:T(8,128)} %convolution_bitcast_fusion.8) | copy-start | bytes 884740
  279.5 43.7 %copy-start.55 = (f32[36,2048]{1,0:T(8,128)S(1)}, f32[36,2048]{1,0:T(8,128)}, u32[]{:S(2)}) copy-start(f32[36,2048]{1,0:T(8,128)} %convolution_bitcast_fusion.6) | copy-start | bytes 884740
  279.5 43.7 %copy-start.56 = (f32[36,2048]{1,0:T(8,128)S(1)}, f32[36,2048]{1,0:T(8,128)}, u32[]{:S(2)}) copy-start(f32[36,2048]{1,0:T(8,128)} %convolution_bitcast_fusion.5) | copy-start | bytes 884740
  324.9 189.7 %copy-start.46 = (f32[2,36,12,36]{3,2,0,1:T(8,128)S(1)}, f32[2,36,12,36]{3,2,0,1:T(8,128)}, u32[]{:S(2)}) copy-start(f32[2,36,12,36]{3,2,0,1:T(8,128)} %reshape.325) | copy-start | bytes 373252
  324.9 189.7 %copy-start.47 = (f32[2,36,12,36]{3,2,0,1:T(8,128)S(1)}, f32[2,36,12,36]{3,2,0,1:T(8,128)}, u32[]{:S(2)}) copy-start(f32[2,36,12,36]{3,2,0,1:T(8,128)} %reshape.327) | copy-start | bytes 373252
  (88 other events, 195.2 us)
Sparse Core Ops, SparseCore 0:
  32.3 286.7 all-reduce.6
  323.2 190.2 all-reduce.8
where the time goes:
time: 644 us; the launch traced here: 637 us
  waiting for transfers between devices  245 us (38%)
  local copies, waits for them, and re-layouts  174 us (27%)
  blocking collectives  105 us (16%)
  matrix products  58.9 us (9%)
  starting transfers between devices  32 us (5%)
  between operations  15.8 us (2%)
    unnamed x4, waiting for transfers between devices  227 us
    reshape x54, local copies, waits for them, and re-layouts, convolve(): summed = summed + matmul(block, window.reshape(C, rows_out * cols_out * Z))  82.9 us
    slice x60, local copies, waits for them, and re-layouts, convolve(): padded[:, shift_x:shift_x + rows_out, shift_y:shift_y + cols_out, shift_z...  72 us
    all_gather x1, blocking collectives, on_device(): shard_piece = lax.all_gather(joined_back, 'gx', axis=0, tiled=True)  63.2 us
    dot_general x66, matrix products, matmul(): return jnp.dot(left, right, precision=highest)  56.6 us
    all_gather x1, blocking collectives, on_device(): shard_piece = lax.all_gather(mixed, 'gy', axis=0, tiled=True)  42.2 us
    ppermute x4, waiting for transfers between devices, with_halo(): lax.ppermute(head, axis, [((i + 1) % count, i) for i in range(ends)])  18.2 us
    ppermute x4, starting transfers between devices, with_halo(): lax.ppermute(tail, axis, [(i, (i + 1) % count) for i in range(ends)])  17.3 us
  transfers between devices with their start and end apart: 10, of which 5 were waited for; matrix products, arithmetic and copies ran while one was open for 35% of the time, Pallas kernels for 0%

commit v1 on v0

--- a/solution.py
+++ b/solution.py
@@ -131,7 +131,9 @@
         ],
         axis=2,
     )
-    shard_piece = lax.all_gather(mixed, "gy", axis=0, tiled=True)
+    shard_piece = jnp.concatenate(
+        lax.all_to_all(jnp.stack([mixed] * lax.axis_size("gy")), "gy", 0, 0), axis=0
+    )
     frequency = y_freqs
     cosine, sine_part = angle_table(local_y, frequency, total_y)
     piece_real = shard_piece[..., :chan_modes]

time: 644 us -> 619 us (0.961)
  blocking collectives: 105 us -> 59.2 us
  local copies, waits for them, and re-layouts: 174 us -> 213 us
  waiting for transfers between devices: 245 us -> 216 us
  starting transfers between devices: 32 us -> 39 us
    all_gather x1 -> x0, blocking collectives: 42.2 us -> none  [on_device(): shard_piece = lax.all_gather(mixed, 'gy', axis=0, tiled=True)]
    unnamed x4, waiting for transfers between devices: 227 us -> 188 us
    slice x60, local copies, waits for them, and re-layouts: 72 us -> 99.4 us  [convolve(): padded[:, shift_x:shift_x + rows_out, shift_y:shift_y + cols_out, shift_z...]
    reshape x54, local copies, waits for them, and re-layouts: 82.9 us -> 93.2 us  [convolve(): summed = summed + matmul(block, window.reshape(C, rows_out * cols_out * Z))]
    all_to_all x0 -> x1, waiting for transfers between devices: none -> 9.42 us  [on_device(): lax.all_to_all(jnp.stack([mixed] * lax.axis_size('gy')), 'gy', 0, 0)]
    all_to_all x0 -> x1, starting transfers between devices: none -> 7.1 us  [on_device(): lax.all_to_all(jnp.stack([mixed] * lax.axis_size('gy')), 'gy', 0, 0)]
  transfers between devices with their start and end apart: 10 -> 11, of which waited for: 5 -> 5; matrix products, arithmetic and copies ran while one was open for 35% -> 43% of each run, Pallas kernels for 0% -> 0%
where the time goes in v1:
time: 619 us; the launch traced here: 612 us
  waiting for transfers between devices  216 us (35%)
  local copies, waits for them, and re-layouts  213 us (34%)
  matrix products  63.8 us (10%)
  blocking collectives  59.2 us (10%)
  starting transfers between devices  39 us (6%)
  between operations  15.5 us (3%)
    unnamed x4, waiting for transfers between devices  188 us
    slice x60, local copies, waits for them, and re-layouts, convolve(): padded[:, shift_x:shift_x + rows_out, shift_y:shift_y + cols_out, shift_z...  99.4 us
    reshape x54, local copies, waits for them, and re-layouts, convolve(): summed = summed + matmul(block, window.reshape(C, rows_out * cols_out * Z))  93.2 us
    dot_general x66, matrix products, matmul(): return jnp.dot(left, right, precision=highest)  61.5 us
    all_gather x1, blocking collectives, on_device(): shard_piece = lax.all_gather(joined_back, 'gx', axis=0, tiled=True)  59.2 us
    ppermute x4, waiting for transfers between devices, with_halo(): lax.ppermute(head, axis, [((i + 1) % count, i) for i in range(ends)])  18.1 us
    ppermute x4, starting transfers between devices, with_halo(): lax.ppermute(tail, axis, [(i, (i + 1) % count) for i in range(ends)])  17.1 us
    ppermute x4, starting transfers between devices, with_halo(): lax.ppermute(head, axis, [((i + 1) % count, i) for i in range(ends)])  14.2 us
  transfers between devices with their start and end apart: 11, of which 5 were waited for; matrix products, arithmetic and copies ran while one was open for 43% of the time, Pallas kernels for 0%

profile of v1, /device:TPU:1, one launch (start us, length us, event | category | flops | bytes accessed | tf_op | source)
XLA Modules:
  0.0 611.7 jit_solution(13462743795642839042)
XLA Ops:
  7.5 8.8 %collective-permute-start.1 = (f32[1,8,2304]{2,1,0:T(8,128)S(1)}, f32[1,8,2304]{2,1,0:T(8,128)S(1)}, u32[]{:S(2)}, u32[]{:S(2)}) collective-permute-start(f32[1,8,2304]{2,1,0:T(8,128)S(1)} %get-tuple-element.75), channel_id=1, source_target_pairs={{16,0},{32,16},{48,32},{64,48},{80,64},{96,80},{112,96},{128,112},... | collective-permute-start | bytes 221192 | tf_op jit(solution)/shard_map/ppermute | solution.py:25
  24.9 5.0 collective-permute-start.2
  32.8 10.6 %collective-permute-done.3 = f32[6,1,2304]{2,1,0:T(1,128)S(1)} collective-permute-done((f32[6,1,2304]{2,1,0:T(1,128)S(1)}, f32[6,1,2304]{2,1,0:T(1,128)S(1)}, u32[]{:S(2)}, u32[]{:S(2)}) %collective-permute-start.3) | collective-permute-done | bytes 55328 | tf_op jit(solution)/shard_map/ppermute | solution.py:25
  46.2 4.2 pad_slice_fusion.24
  50.5 3.9 fusion.326
  68.2 2.3 copy.77
  89.2 2.3 copy.82
  96.6 2.3 copy.85
  171.1 2.4 collective-permute-start.5
  173.6 3.7 collective-permute-done.5
  177.4 8.3 %collective-permute-start.6 = (f32[6,1,2304]{2,1,0:T(1,128)S(1)}, f32[6,1,2304]{2,1,0:T(1,128)S(1)}, u32[]{:S(2)}, u32[]{:S(2)}) collective-permute-start(f32[6,1,2304]{2,1,0:T(1,128)S(1)} %get-tuple-element.69), channel_id=1, source_target_pairs={{0,1},{1,2},{2,3},{3,4},{4,5},{5,6},{6,7},{7,8},{8,9},{9,10},{10,1... | collective-permute-start | bytes 165896 | tf_op jit(solution)/shard_map/ppermute | solution.py:23
  192.9 3.7 collective-permute-done.7
  199.5 4.1 pad_slice_fusion.6
  203.6 4.0 fusion.324
  208.2 2.3 copy.116
  223.2 2.3 copy.106
  238.2 2.4 copy.112
  245.7 2.3 copy.115
  253.3 2.3 copy.118
  268.6 2.4 copy.120
  324.0 188.0 %all-reduce.9.cloned.1.call-done = f32[32,1,864]{2,0,1:T(8,128)} async-done(((f32[32,1,864]{2,0,1:T(8,128)}), f32[32,1,864]{2,0,1:T(8,128)}) %all-reduce.9.cloned.1.call-update) | async-done | bytes 110608
  515.0 7.1 %all-to-all-start = ((f32[16,2,1,864]{3,2,1,0:T(1,128)}), f32[16,2,1,864]{3,2,1,0:T(1,128)S(1)}, u32[]{:S(2)}, u32[]{:S(2)}) async-start(f32[16,2,1,864]{3,2,1,0:T(1,128)} %stack.2), calls=%async_computation | async-start | bytes 229376 | tf_op jit(solution)/shard_map/all_to_all | solution.py:135
  526.9 9.4 %all-to-all-done = f32[16,2,1,864]{3,2,1,0:T(1,128)S(1)} async-done(((f32[16,2,1,864]{3,2,1,0:T(1,128)}), f32[16,2,1,864]{3,2,1,0:T(1,128)S(1)}, u32[]{:S(2)}, u32[]{:S(2)}) %all-to-all-start) | async-done | bytes 110624 | tf_op jit(solution)/shard_map/all_to_all | solution.py:135
  537.8 59.2 %all-gather = f32[32,1,6912]{2,1,0:T(1,128)S(1)} all-gather(f32[1,1,6912]{2,1,0:T(1,128)S(1)} %maximum_bitcast_fusion), channel_id=1, replica_groups=mesh['gx'=32,'gy'=16] {'gx'}, dimensions={0}, use_global_device_ids=true | all-gather | bytes 912384 | tf_op jit(solution)/shard_map/all_gather | solution.py:151
  (409 shorter events, 252.6 us)
Async XLA Ops:
  6.5 311.7 %all-reduce.7.cloned.1.call-start = ((), (), s32[]{:S(2)}) async-start(), calls=%async_computation.1 | async-start | bytes 1769472
  7.5 17.3 %collective-permute-start.1 = (f32[1,8,2304]{2,1,0:T(8,128)S(1)}, f32[1,8,2304]{2,1,0:T(8,128)S(1)}, u32[]{:S(2)}, u32[]{:S(2)}) collective-permute-start(f32[1,8,2304]{2,1,0:T(8,128)S(1)} %get-tuple-element.75), channel_id=1, source_target_pairs={{16,0},{32,16},{48,32},{64,48},{80,64},{96,80},{112,96},{128,112},... | collective-permute-start | bytes 221192 | tf_op jit(solution)/shard_map/ppermute | solution.py:25
  16.3 8.5 %collective-permute-start = (f32[1,8,2304]{2,1,0:T(8,128)S(1)}, f32[1,8,2304]{2,1,0:T(8,128)S(1)}, u32[]{:S(2)}, u32[]{:S(2)}) collective-permute-start(f32[1,8,2304]{2,1,0:T(8,128)S(1)} %get-tuple-element.76), channel_id=1, source_target_pairs={{0,16},{16,32},{32,48},{48,64},{64,80},{80,96},{96,112},{112,128},... | collective-permute-start | bytes 221192 | tf_op jit(solution)/shard_map/ppermute | solution.py:23
  24.9 7.9 %collective-permute-start.2 = (f32[6,1,2304]{2,1,0:T(1,128)S(1)}, f32[6,1,2304]{2,1,0:T(1,128)S(1)}, u32[]{:S(2)}, u32[]{:S(2)}) collective-permute-start(f32[6,1,2304]{2,1,0:T(1,128)S(1)} %get-tuple-element.71), channel_id=1, source_target_pairs={{0,1},{1,2},{2,3},{3,4},{4,5},{5,6},{6,7},{7,8},{8,9},{9,10},{10,1... | collective-permute-start | bytes 165896 | tf_op jit(solution)/shard_map/ppermute | solution.py:23
  29.9 13.5 %collective-permute-start.3 = (f32[6,1,2304]{2,1,0:T(1,128)S(1)}, f32[6,1,2304]{2,1,0:T(1,128)S(1)}, u32[]{:S(2)}, u32[]{:S(2)}) collective-permute-start(f32[6,1,2304]{2,1,0:T(1,128)S(1)} %get-tuple-element.72), channel_id=1, source_target_pairs={{1,0},{2,1},{3,2},{4,3},{5,4},{6,5},{7,6},{8,7},{9,8},{10,9},{11,1... | collective-permute-start | bytes 165896 | tf_op jit(solution)/shard_map/ppermute | solution.py:25
  32.2 479.8 %all-reduce.9.cloned.1.call-start = ((), (), s32[]{:S(2)}) async-start(), calls=%async_computation.2 | async-start | bytes 229376
  104.1 4.5 copy-start.12
  168.8 21.2 %copy-start.74 = (f32[1,2,36,432]{3,1,2,0:T(2,128)S(1)}, f32[1,2,36,432]{3,1,2,0:T(2,128)}, u32[]{:S(2)}) copy-start(f32[1,2,36,432]{3,1,2,0:T(2,128)} %param.8) | copy-start | bytes 373252
  168.9 4.6 collective-permute-start.4
  171.0 20.2 %copy-start.75 = (f32[1,2,36,432]{3,1,2,0:T(2,128)S(1)}, f32[1,2,36,432]{3,1,2,0:T(2,128)}, u32[]{:S(2)}) copy-start(f32[1,2,36,432]{3,1,2,0:T(2,128)} %param.9) | copy-start | bytes 373252
  171.1 6.2 %collective-permute-start.5 = (f32[1,8,2304]{2,1,0:T(8,128)S(1)}, f32[1,8,2304]{2,1,0:T(8,128)S(1)}, u32[]{:S(2)}, u32[]{:S(2)}) collective-permute-start(f32[1,8,2304]{2,1,0:T(8,128)S(1)} %slice.465), channel_id=1, source_target_pairs={{16,0},{32,16},{48,32},{64,48},{80,64},{96,80},{112,96},{128,112},... | collective-permute-start | bytes 221192 | tf_op jit(solution)/shard_map/ppermute | solution.py:25
  177.4 15.5 %collective-permute-start.6 = (f32[6,1,2304]{2,1,0:T(1,128)S(1)}, f32[6,1,2304]{2,1,0:T(1,128)S(1)}, u32[]{:S(2)}, u32[]{:S(2)}) collective-permute-start(f32[6,1,2304]{2,1,0:T(1,128)S(1)} %get-tuple-element.69), channel_id=1, source_target_pairs={{0,1},{1,2},{2,3},{3,4},{4,5},{5,6},{6,7},{7,8},{8,9},{9,10},{10,1... | collective-permute-start | bytes 165896 | tf_op jit(solution)/shard_map/ppermute | solution.py:23
  185.7 10.9 %collective-permute-start.7 = (f32[6,1,2304]{2,1,0:T(1,128)S(1)}, f32[6,1,2304]{2,1,0:T(1,128)S(1)}, u32[]{:S(2)}, u32[]{:S(2)}) collective-permute-start(f32[6,1,2304]{2,1,0:T(1,128)S(1)} %get-tuple-element.70), channel_id=1, source_target_pairs={{1,0},{2,1},{3,2},{4,3},{5,4},{6,5},{7,6},{8,7},{9,8},{10,9},{11,1... | collective-permute-start | bytes 165896 | tf_op jit(solution)/shard_map/ppermute | solution.py:25
  238.2 4.4 copy-start.17
  253.3 4.5 copy-start.13
  259.0 6.4 %copy-start.11 = (f32[36,4,8,64]{3,0,1,2:T(8,128)S(1)}, f32[36,4,8,64]{3,0,1,2:T(8,128)}, u32[]{:S(2)}) copy-start(f32[36,4,8,64]{3,0,1,2:T(8,128)} %get-tuple-element.23) | copy-start | bytes 884740
  268.6 4.4 copy-start.9
  276.1 6.4 %copy-start.7 = (f32[36,4,8,64]{3,0,1,2:T(8,128)S(1)}, f32[36,4,8,64]{3,0,1,2:T(8,128)}, u32[]{:S(2)}) copy-start(f32[36,4,8,64]{3,0,1,2:T(8,128)} %get-tuple-element.27) | copy-start | bytes 884740
  286.1 6.4 %copy-start.4 = (f32[36,4,8,64]{3,0,1,2:T(8,128)S(1)}, f32[36,4,8,64]{3,0,1,2:T(8,128)}, u32[]{:S(2)}) copy-start(f32[36,4,8,64]{3,0,1,2:T(8,128)} %get-tuple-element.29) | copy-start | bytes 884740
  296.2 6.4 %copy-start.1 = (f32[36,4,8,64]{3,0,1,2:T(8,128)S(1)}, f32[36,4,8,64]{3,0,1,2:T(8,128)}, u32[]{:S(2)}) copy-start(f32[36,4,8,64]{3,0,1,2:T(8,128)} %get-tuple-element.31) | copy-start | bytes 884740
  317.0 5.2 copy-start.70
  323.4 189.7 %copy-start.27 = (f32[2,36,12,36]{3,2,0,1:T(8,128)S(1)}, f32[2,36,12,36]{3,2,0,1:T(8,128)}, u32[]{:S(2)}) copy-start(f32[2,36,12,36]{3,2,0,1:T(8,128)} %reshape.331) | copy-start | bytes 373252
  323.4 189.7 %copy-start.28 = (f32[2,36,12,36]{3,2,0,1:T(8,128)S(1)}, f32[2,36,12,36]{3,2,0,1:T(8,128)}, u32[]{:S(2)}) copy-start(f32[2,36,12,36]{3,2,0,1:T(8,128)} %reshape.333) | copy-start | bytes 373252
  515.0 21.3 %all-to-all-start = ((f32[16,2,1,864]{3,2,1,0:T(1,128)}), f32[16,2,1,864]{3,2,1,0:T(1,128)S(1)}, u32[]{:S(2)}, u32[]{:S(2)}) async-start(f32[16,2,1,864]{3,2,1,0:T(1,128)} %stack.2), calls=%async_computation | async-start | bytes 229376 | tf_op jit(solution)/shard_map/all_to_all | solution.py:135
  (63 other events, 138.4 us)
Sparse Core Ops, SparseCore 0:
  32.3 285.0 all-reduce.6
  322.3 189.6 all-reduce.8
